TPU v7x, 32 devices: a whole 2x2x4 slice. The times are simulated.
32 devices in a mesh: dp: 4 (over y, x), seq: 8 (over z, core).
Axes of the slice: x: 2, y: 2, z: 4, core: 2. Of those that a mesh axis runs over, the one named last changes fastest.
Arguments:
- tokens: bfloat16 [16384, 1024], P(('dp', 'seq')), may hold values from -6 to 6
- doc_lengths: int32 [4, 3], P('dp'), may hold values from 1 to 4094, as said below
- norm_gain: bfloat16 [1024], replicated, may hold values from 0.5 to 1.5
- w_qkv: bfloat16 [1024, 3072], P(('dp', 'seq')), may hold values from -0.1875 to 0.1875
- w_beta: bfloat16 [1024, 8], P(('dp', 'seq')), may hold values from -0.375 to 0.375
- conv_weight: bfloat16 [4, 3072], replicated, may hold values from -3 to 3
- head_gain: bfloat16 [128], replicated, may hold values from 0.5 to 1.5
- w_out: bfloat16 [1024, 1024], P(('dp', 'seq')), may hold values from -0.1875 to 0.1875
- mlp_gain: bfloat16 [1024], replicated, may hold values from 0.5 to 1.5
- w_mlp_in: bfloat16 [1024, 5632], P(('dp', 'seq')), may hold values from -0.1875 to 0.1875
- w_down: bfloat16 [2816, 1024], P(('dp', 'seq')), may hold values from -0.109375 to 0.109375
- grad_out: bfloat16 [16384, 1024], P(('dp', 'seq')), may hold values from -6 to 6
Outputs:
- out: bfloat16 [16384, 1024], P(('dp', 'seq'))
- grad_tokens: bfloat16 [16384, 1024], P(('dp', 'seq'))
- grad_norm_gain: float32 [1024], replicated
- grad_w_qkv: float32 [1024, 3072], P(('dp', 'seq'))
- grad_w_beta: float32 [1024, 8], P(('dp', 'seq'))
- grad_conv: float32 [4, 3072], replicated
- grad_head_gain: float32 [128], replicated
- grad_w_out: float32 [1024, 1024], P(('dp', 'seq'))
- grad_mlp_gain: float32 [1024], replicated
- grad_w_mlp_in: float32 [1024, 5632], P(('dp', 'seq'))
- grad_w_down: float32 [2816, 1024], P(('dp', 'seq'))
Inputs may be any that keep to these rules, and one draw needn't show every extreme that they name: `doc_lengths`: each row holds, in order, the lengths of the three documents packed into one group's 4096 tokens; the first and the last are each shorter than 512.
All inputs are finite; a program needn't handle non-finite values.
Results may differ from a plain program's by a relative error of at most 0.015.
Values may be sent and summed in bfloat16 or wider, within the bound.
A program may use at most 320 MiB of HBM per device.

v0:
```python
import jax
import jax.numpy as jnp
from jax import lax
from jax.sharding import PartitionSpec as P

norm_eps = 1e-05
unit_eps = 1e-06
block_rows = 64
highest = lax.Precision.HIGHEST


def from_behind(value, axis, steps):
    count = lax.axis_size(axis)
    first, last = (max(0, -steps), min(count, count - steps))
    return lax.ppermute(value, axis, [(source, source + steps) for source in range(first, last)])


def shortened(shard):

    def short(part):
        return part.astype(jnp.bfloat16) if part.dtype == jnp.float32 else part

    return jax.tree.map(short, shard)


def rms_scale(values, gain):
    return values * lax.rsqrt(jnp.mean(values * values, axis=-1, keepdims=True) + norm_eps) * gain


def doc_ids(lengths, positions):
    ends = jnp.cumsum(lengths)
    inside = (positions[:, None] >= ends[None, :]).astype(jnp.int32)
    return jnp.where(positions >= 0, jnp.sum(inside, axis=1), -1)


def short_conv(padded, weight, docs_pad):
    kernel = weight.shape[0]
    row_count = padded.shape[0] - kernel + 1
    total = jnp.zeros((row_count, padded.shape[1]), jnp.float32)
    for offset in range(kernel):
        keep = (docs_pad[offset : offset + row_count] == docs_pad[kernel - 1 :]).astype(jnp.float32)
        total = total + weight[offset] * padded[offset : offset + row_count] * keep[:, None]
    return total


def features(padded, weight, logits, docs_pad):
    mixed = jax.nn.silu(short_conv(padded, weight, docs_pad))
    row_count = mixed.shape[0]
    heads = logits.shape[1]
    mixed = mixed.reshape(row_count, 3, heads, -1)
    width = mixed.shape[-1]
    query = mixed[:, 0]
    keyed = mixed[:, 1]
    value = mixed[:, 2]
    query = (
        query
        * lax.rsqrt(jnp.sum(query * query, axis=-1, keepdims=True) + unit_eps)
        * width ** (-0.5)
    )
    keyed = keyed * lax.rsqrt(jnp.sum(keyed * keyed, axis=-1, keepdims=True) + unit_eps)
    return (query, keyed, value, jax.nn.sigmoid(logits))


def swiglu(gate_up):
    half = gate_up.shape[1] // 2
    return jax.nn.silu(gate_up[:, :half]) * gate_up[:, half:]


def delta_pass(state, query, keyed, values, beta, docs, prev_doc, with_out):
    row_count, heads, width = keyed.shape
    extent = values.shape[-1]
    block = min(block_rows, row_count)
    blocks = row_count // block
    before = jnp.concatenate([prev_doc[None], docs[:-1]])
    first_prev = before.reshape(blocks, block)[:, 0]

    def split_rows(array):
        shaped = array.reshape((blocks, block) + array.shape[1:])
        return jnp.swapaxes(shaped, 1, 2)

    pieces = (
        split_rows(query),
        split_rows(keyed),
        split_rows(values),
        split_rows(beta),
        docs.reshape(blocks, block),
        first_prev,
    )
    row_index = lax.broadcasted_iota(jnp.int32, (block, block), 0)
    col_index = lax.broadcasted_iota(jnp.int32, (block, block), 1)
    identity = jnp.eye(block, dtype=jnp.float32)

    def advance(carried, inputs_now):
        query_block, key_block, value_block, beta_block, doc_block, doc_before = inputs_now
        same_doc = doc_block[:, None] == doc_block[None, :]
        strictly = (same_doc & (row_index > col_index)).astype(jnp.float32)
        inclusive = (same_doc & (row_index >= col_index)).astype(jnp.float32)
        continuing = (doc_block == doc_before).astype(jnp.float32)
        last_doc = (doc_block == doc_block[-1]).astype(jnp.float32)
        key_gram = jnp.einsum("hck,hdk->hcd", key_block, key_block, precision=highest)
        lower_mat = identity + key_gram * beta_block[:, :, None] * strictly
        right_side = jnp.concatenate(
            [
                beta_block[:, :, None] * value_block,
                (beta_block * continuing[None, :])[:, :, None] * key_block,
            ],
            axis=-1,
        )
        solved = lax.linalg.triangular_solve(
            lower_mat, right_side, left_side=True, lower=True, unit_diagonal=True
        )
        fresh_rows = solved[..., :extent] - jnp.einsum(
            "hck,hrk->hcr", solved[..., extent:], carried, precision=highest
        )
        updated = carried * continuing[-1] + jnp.einsum(
            "hcr,hck->hrk", fresh_rows * last_doc[None, :, None], key_block, precision=highest
        )
        if with_out:
            scores = (
                jnp.einsum("hck,hdk->hcd", query_block, key_block, precision=highest) * inclusive
            )
            result = continuing[None, :, None] * jnp.einsum(
                "hck,hrk->hcr", query_block, carried, precision=highest
            )
            result = result + jnp.einsum("hcd,hdr->hcr", scores, fresh_rows, precision=highest)
            return (updated, result)
        return (updated, None)

    ending, results = lax.scan(advance, state, pieces)
    if with_out:
        results = jnp.swapaxes(results, 1, 2).reshape(row_count, heads, extent)
    return (results, ending)


def contract_rows(left, right):
    return lax.dot_general(
        left, right, (((0,), (0,)), ((), ())), preferred_element_type=jnp.float32
    )


def contract_cols(left, right):
    return lax.dot_general(
        left, right, (((1,), (1,)), ((), ())), preferred_element_type=jnp.float32
    )


def local(
    tokens,
    doc_lengths,
    norm_gain,
    w_qkv,
    w_beta,
    conv_weight,
    head_gain,
    w_out,
    mlp_gain,
    w_mlp_in,
    w_down,
    grad_out,
):
    row_count, model_width = tokens.shape
    heads = w_beta.shape[1]
    width = head_gain.shape[0]
    kernel = conv_weight.shape[0]
    qkv_width = w_qkv.shape[1]
    conv_taps = conv_weight.astype(jnp.float32)
    weights = (
        lax.all_gather(w_qkv, ("dp", "seq"), axis=0, tiled=True),
        lax.all_gather(w_beta, ("dp", "seq"), axis=0, tiled=True),
        lax.all_gather(w_out, ("dp", "seq"), axis=0, tiled=True),
        lax.all_gather(w_mlp_in, ("dp", "seq"), axis=0, tiled=True),
    )
    inputs = tokens.astype(jnp.float32)
    norm_one, pull_one = jax.vjp(rms_scale, inputs, norm_gain.astype(jnp.float32))
    xn1 = norm_one.astype(jnp.bfloat16)
    projected = jnp.dot(xn1, weights[0], preferred_element_type=jnp.float32)
    logits = jnp.dot(xn1, weights[1], preferred_element_type=jnp.float32)
    start = lax.axis_index("seq") * row_count
    positions = start - (kernel - 1) + jnp.arange(row_count + kernel - 1, dtype=jnp.int32)
    docs_pad = doc_ids(doc_lengths[0], positions)
    docs = docs_pad[kernel - 1 :]
    prev_doc = docs_pad[kernel - 2]
    received = from_behind(
        projected[row_count - kernel + 1 :].astype(jnp.bfloat16), "seq", 1
    ).astype(jnp.float32)
    padded = jnp.concatenate([received, projected], axis=0)

    def feature_fn(padded_rows, taps, logit_rows):
        return features(padded_rows, taps, logit_rows, docs_pad)

    (query, keyed, value, beta), pull_feat = jax.vjp(feature_fn, padded, conv_taps, logits)
    zero_state = jnp.zeros((heads, width, width), jnp.float32)
    unit_map = jnp.broadcast_to(jnp.eye(width, dtype=jnp.float32), (heads, width, width))
    _, stacked = delta_pass(
        jnp.concatenate([zero_state, unit_map], axis=1),
        query,
        keyed,
        jnp.concatenate([value, jnp.zeros_like(value)], axis=-1),
        beta,
        docs,
        prev_doc,
        False,
    )
    fresh_state = stacked[:, :width]
    decay_map = stacked[:, width:]

    def relay_step(turn, pair):
        moved = from_behind(pair[1].astype(jnp.bfloat16), "seq", 1).astype(jnp.float32)
        return (
            moved,
            jnp.einsum("hij,hjk->hik", moved, decay_map, precision=highest) + fresh_state,
        )

    state_in, _ = lax.fori_loop(0, lax.axis_size("seq") - 1, relay_step, (zero_state, fresh_state))

    def segment_rule(initial, query_rows, key_rows, value_rows, beta_rows):
        return delta_pass(
            initial, query_rows, key_rows, value_rows, beta_rows, docs, prev_doc, True
        )

    (mixed, state_end), pull_rule = jax.vjp(segment_rule, state_in, query, keyed, value, beta)
    head_norm, pull_head = jax.vjp(rms_scale, mixed, head_gain.astype(jnp.float32))
    head_out = head_norm.reshape(row_count, model_width).astype(jnp.bfloat16)
    hidden_one = inputs + jnp.dot(head_out, weights[2], preferred_element_type=jnp.float32)
    norm_two, pull_two = jax.vjp(rms_scale, hidden_one, mlp_gain.astype(jnp.float32))
    xn2 = norm_two.astype(jnp.bfloat16)
    gate_up = jnp.dot(xn2, weights[3], preferred_element_type=jnp.float32)
    hidden_f, pull_act = jax.vjp(swiglu, gate_up)
    hidden = hidden_f.astype(jnp.bfloat16)
    mlp_out = jnp.dot(
        hidden,
        lax.all_gather(w_down, ("dp", "seq"), axis=0, tiled=True),
        preferred_element_type=jnp.float32,
    )
    out = (hidden_one + mlp_out).astype(jnp.bfloat16)
    grad_in = grad_out.astype(jnp.float32)
    d_hidden = contract_cols(grad_out, lax.all_gather(w_down, ("dp", "seq"), axis=0, tiled=True))
    back_weights = (
        lax.all_gather(w_qkv, ("dp", "seq"), axis=0, tiled=True),
        lax.all_gather(w_beta, ("dp", "seq"), axis=0, tiled=True),
        lax.all_gather(w_out, ("dp", "seq"), axis=0, tiled=True),
        lax.all_gather(w_mlp_in, ("dp", "seq"), axis=0, tiled=True),
    )
    d_gate_up = pull_act(d_hidden)[0].astype(jnp.bfloat16)
    d_norm_two = contract_cols(d_gate_up, back_weights[3])
    d_from_two, d_mlp_gain = pull_two(d_norm_two)
    d_hidden_one = grad_in + d_from_two
    d_att = d_hidden_one.astype(jnp.bfloat16)
    d_head = contract_cols(d_att, back_weights[2])
    d_mixed, d_head_gain = pull_head(d_head.reshape(row_count, heads, width))
    seed = pull_rule((d_mixed, jnp.zeros_like(state_end)))[0]
    flipped = jnp.swapaxes(decay_map, 1, 2)

    def return_step(turn, pair):
        moved = from_behind(pair[1].astype(jnp.bfloat16), "seq", -1).astype(jnp.float32)
        return (moved, jnp.einsum("hij,hjk->hik", moved, flipped, precision=highest) + seed)

    grad_end, _ = lax.fori_loop(0, lax.axis_size("seq") - 1, return_step, (zero_state, seed))
    _, d_query, d_key, d_value, d_beta = pull_rule((d_mixed, grad_end))
    d_padded, d_conv, d_logits = pull_feat((d_query, d_key, d_value, d_beta))
    returned = from_behind(shortened(d_padded[: kernel - 1]), "seq", -1)
    d_projected = d_padded[kernel - 1 :] + jnp.concatenate(
        [jnp.zeros((row_count - kernel + 1, qkv_width), jnp.float32), returned], axis=0
    )
    d_proj_b = d_projected.astype(jnp.bfloat16)
    d_logit_b = d_logits.astype(jnp.bfloat16)
    d_norm_one = contract_cols(d_proj_b, back_weights[0]) + contract_cols(
        d_logit_b, back_weights[1]
    )
    d_from_one, d_norm_gain = pull_one(d_norm_one)
    grad_tokens = (d_hidden_one + d_from_one).astype(jnp.bfloat16)
    row_grads = (
        lax.psum_scatter(
            contract_rows(xn1, d_proj_b), ("dp", "seq"), scatter_dimension=0, tiled=True
        ),
        lax.psum_scatter(
            contract_rows(xn1, d_logit_b), ("dp", "seq"), scatter_dimension=0, tiled=True
        ),
        lax.psum_scatter(
            contract_rows(head_out, d_att), ("dp", "seq"), scatter_dimension=0, tiled=True
        ),
        lax.psum_scatter(
            contract_rows(xn2, d_gate_up), ("dp", "seq"), scatter_dimension=0, tiled=True
        ),
    )
    grad_w_down = lax.psum_scatter(
        contract_rows(hidden, grad_out), ("dp", "seq"), scatter_dimension=0, tiled=True
    )
    small_sums = lax.psum((d_norm_gain, d_conv, d_head_gain, d_mlp_gain), ("dp", "seq"))
    return (
        out,
        grad_tokens,
        small_sums[0],
        row_grads[0],
        row_grads[1],
        small_sums[1],
        small_sums[2],
        row_grads[2],
        small_sums[3],
        row_grads[3],
        grad_w_down,
    )


def solution(mesh):
    placed = (
        P(("dp", "seq"), None),
        P("dp", None),
        P(),
        P(("dp", "seq"), None),
        P(("dp", "seq"), None),
        P(),
        P(),
        P(("dp", "seq"), None),
        P(),
        P(("dp", "seq"), None),
        P(("dp", "seq"), None),
        P(("dp", "seq"), None),
    )
    return jax.shard_map(
        local,
        mesh=mesh,
        in_specs=placed,
        out_specs=(
            P(("dp", "seq"), None),
            P(("dp", "seq"), None),
            P(),
            P(("dp", "seq"), None),
            P(("dp", "seq"), None),
            P(),
            P(),
            P(("dp", "seq"), None),
            P(),
            P(("dp", "seq"), None),
            P(("dp", "seq"), None),
        ),
        check_vma=False,
    )
```

profile of v0, /device:TPU:0, one launch (start us, length us, event | category | flops | bytes accessed | tf_op | source)
XLA Modules:
  0.0 2855.2 jit_solution(16780564698505942755)
XLA Ops:
  15.1 43.7 %all-gather = bf16[32,32,8]{1,2,0:T(8,128)(2,1)S(1)} all-gather(bf16[1,32,8]{1,2,0:T(8,128)(2,1)S(1)} %bitcast.650), channel_id=1, replica_groups=mesh['dp'=4,'seq'=8] {'dp','seq'}, dimensions={0}, use_global_device_ids=true | all-gather | bytes 16896 | tf_op jit(solution)/shard_map/all_gather | solution.py:169
  59.5 23.9 all-gather.6.cloned.1.call-done
  94.9 13.9 multiply_bitcast_fusion.1
  119.6 433.3 %while.126 = (s32[]{:T(128)}, f32[8,256,128]{2,1,0:T(8,128)S(1)}, s32[8,64]{1,0:T(8,128)S(1)}, s32[8]{0:T(128)S(1)}, f32[8,8,64,128]{3,2,1,0:T(8,128)S(1)}, /*in...) while((s32[]{:T(128)}, f32[8,256,128]{2,1,0:T(8,128)S(1)}, ...), condition=%wide.region_5.6_spmd.clone, body=%wide.region_4.5_spmd.clone.sunk | while | flops 605361024 | bytes 10138592 | solution.py:129
  125.2 40.7 %custom-call.46 = f32[8,1,64,64]{2,3,1,0:T(8,128)} custom-call(f32[8,1,64,64]{3,2,1,0:T(8,128)} %fusion.364), custom_call_target="InvertDiagBlocksLowerTriangular" | custom-call | tf_op jit(solution)/shard_map/while/body/eval_jaxpr/triangular_solve | solution.py:109
  179.4 40.7 %custom-call.46 = f32[8,1,64,64]{2,3,1,0:T(8,128)} custom-call(f32[8,1,64,64]{3,2,1,0:T(8,128)} %fusion.364), custom_call_target="InvertDiagBlocksLowerTriangular" | custom-call | tf_op jit(solution)/shard_map/while/body/eval_jaxpr/triangular_solve | solution.py:109
  233.6 40.7 %custom-call.46 = f32[8,1,64,64]{2,3,1,0:T(8,128)} custom-call(f32[8,1,64,64]{3,2,1,0:T(8,128)} %fusion.364), custom_call_target="InvertDiagBlocksLowerTriangular" | custom-call | tf_op jit(solution)/shard_map/while/body/eval_jaxpr/triangular_solve | solution.py:109
  287.7 40.7 %custom-call.46 = f32[8,1,64,64]{2,3,1,0:T(8,128)} custom-call(f32[8,1,64,64]{3,2,1,0:T(8,128)} %fusion.364), custom_call_target="InvertDiagBlocksLowerTriangular" | custom-call | tf_op jit(solution)/shard_map/while/body/eval_jaxpr/triangular_solve | solution.py:109
  341.9 40.7 %custom-call.46 = f32[8,1,64,64]{2,3,1,0:T(8,128)} custom-call(f32[8,1,64,64]{3,2,1,0:T(8,128)} %fusion.364), custom_call_target="InvertDiagBlocksLowerTriangular" | custom-call | tf_op jit(solution)/shard_map/while/body/eval_jaxpr/triangular_solve | solution.py:109
  396.1 40.7 %custom-call.46 = f32[8,1,64,64]{2,3,1,0:T(8,128)} custom-call(f32[8,1,64,64]{3,2,1,0:T(8,128)} %fusion.364), custom_call_target="InvertDiagBlocksLowerTriangular" | custom-call | tf_op jit(solution)/shard_map/while/body/eval_jaxpr/triangular_solve | solution.py:109
  450.2 40.7 %custom-call.46 = f32[8,1,64,64]{2,3,1,0:T(8,128)} custom-call(f32[8,1,64,64]{3,2,1,0:T(8,128)} %fusion.364), custom_call_target="InvertDiagBlocksLowerTriangular" | custom-call | tf_op jit(solution)/shard_map/while/body/eval_jaxpr/triangular_solve | solution.py:109
  504.4 40.7 %custom-call.46 = f32[8,1,64,64]{2,3,1,0:T(8,128)} custom-call(f32[8,1,64,64]{3,2,1,0:T(8,128)} %fusion.364), custom_call_target="InvertDiagBlocksLowerTriangular" | custom-call | tf_op jit(solution)/shard_map/while/body/eval_jaxpr/triangular_solve | solution.py:109
  561.8 65.5 %while.124 = (s32[]{:T(128)}, f32[8,128,128]{2,1,0:T(8,128)}, bf16[8,128,128]{2,1,0:T(8,128)(2,1)}, f32[8,128,128]{2,1,0:T(8,128)S(1)}, f32[8,128,128]{2,1,0:T(8,128)S(1)}, /*index=5*/s32[]{:T(128)}) while((s32[]{:T(128)}, f32[8,128,128]{2,1,0:T(8,128)}, bf16[8,128,128]{2,1,0:T(8,128)(2,1)}, f32[8,128,128]{2,1,0:T(8,128)S(1)}, ...), condition=%wide.region_7.8_spmd, body=%wide.region_6.7_spmd.sunk | while | flops 201719808 | bytes 3407981 | solution.py:214
  627.3 533.8 %while.128 = (s32[]{:T(128)}, f32[8,128,128]{2,1,0:T(8,128)}, f32[8,8,64,128]{3,2,1,0:T(8,128)}, f32[8,8,64,1]{2,1,3,0:T(8,128)}, f32[8,8,64,64]{3,2,1,0:T(8,128...) while((s32[]{:T(128)}, f32[8,128,128]{2,1,0:T(8,128)}, ...), condition=%wide.region_10.11_spmd.clone.clone, body=%wide.region_9.10_spmd.clone.clone.sunk | while | flops 554874688 | bytes 16839100 | solution.py:129
  640.3 40.7 %custom-call.48 = f32[8,1,64,64]{2,3,1,0:T(8,128)} custom-call(f32[8,1,64,64]{3,2,1,0:T(8,128)} %add_bitcast_fusion.5), custom_call_target="InvertDiagBlocksLowerTriangular" | custom-call | tf_op jit(solution)/shard_map/jvp()/while/body/eval_jaxpr/triangular_solve | solution.py:109
  707.0 40.7 %custom-call.48 = f32[8,1,64,64]{2,3,1,0:T(8,128)} custom-call(f32[8,1,64,64]{3,2,1,0:T(8,128)} %add_bitcast_fusion.5), custom_call_target="InvertDiagBlocksLowerTriangular" | custom-call | tf_op jit(solution)/shard_map/jvp()/while/body/eval_jaxpr/triangular_solve | solution.py:109
  773.8 40.7 %custom-call.48 = f32[8,1,64,64]{2,3,1,0:T(8,128)} custom-call(f32[8,1,64,64]{3,2,1,0:T(8,128)} %add_bitcast_fusion.5), custom_call_target="InvertDiagBlocksLowerTriangular" | custom-call | tf_op jit(solution)/shard_map/jvp()/while/body/eval_jaxpr/triangular_solve | solution.py:109
  840.5 40.7 %custom-call.48 = f32[8,1,64,64]{2,3,1,0:T(8,128)} custom-call(f32[8,1,64,64]{3,2,1,0:T(8,128)} %add_bitcast_fusion.5), custom_call_target="InvertDiagBlocksLowerTriangular" | custom-call | tf_op jit(solution)/shard_map/jvp()/while/body/eval_jaxpr/triangular_solve | solution.py:109
  907.2 40.7 %custom-call.48 = f32[8,1,64,64]{2,3,1,0:T(8,128)} custom-call(f32[8,1,64,64]{3,2,1,0:T(8,128)} %add_bitcast_fusion.5), custom_call_target="InvertDiagBlocksLowerTriangular" | custom-call | tf_op jit(solution)/shard_map/jvp()/while/body/eval_jaxpr/triangular_solve | solution.py:109
  973.9 40.7 %custom-call.48 = f32[8,1,64,64]{2,3,1,0:T(8,128)} custom-call(f32[8,1,64,64]{3,2,1,0:T(8,128)} %add_bitcast_fusion.5), custom_call_target="InvertDiagBlocksLowerTriangular" | custom-call | tf_op jit(solution)/shard_map/jvp()/while/body/eval_jaxpr/triangular_solve | solution.py:109
  1040.6 40.7 %custom-call.48 = f32[8,1,64,64]{2,3,1,0:T(8,128)} custom-call(f32[8,1,64,64]{3,2,1,0:T(8,128)} %add_bitcast_fusion.5), custom_call_target="InvertDiagBlocksLowerTriangular" | custom-call | tf_op jit(solution)/shard_map/jvp()/while/body/eval_jaxpr/triangular_solve | solution.py:109
  1107.4 40.7 %custom-call.48 = f32[8,1,64,64]{2,3,1,0:T(8,128)} custom-call(f32[8,1,64,64]{3,2,1,0:T(8,128)} %add_bitcast_fusion.5), custom_call_target="InvertDiagBlocksLowerTriangular" | custom-call | tf_op jit(solution)/shard_map/jvp()/while/body/eval_jaxpr/triangular_solve | solution.py:109
  1176.3 12.6 fusion.221
  1188.9 13.0 fusion.201
  1202.0 14.4 multiply_reduce_fusion.4
  1227.2 68.6 %while.129 = (s32[]{:T(128)}, f32[8,128,128]{2,1,0:T(8,128)S(1)}, f32[8,1,64,1]{2,3,1,0:T(1,128)S(1)}, f32[8,8,64,128]{3,2,1,0:T(8,128)}, f32[8,8,64,128]{3,2,1,...) while((s32[]{:T(128)}, f32[8,128,128]{2,1,0:T(8,128)S(1)}, ...), condition=%wide.region_16.17_spmd.clone, body=%wide.region_15.16_spmd.clone.sunk | while | flops 353239040 | bytes 5247923 | solution.py:129
  1297.3 69.3 %while.125 = (s32[]{:T(128)}, f32[8,128,128]{2,1,0:T(8,128)}, bf16[8,128,128]{2,1,0:T(8,128)(2,1)}, f32[8,128,128]{2,1,0:T(8,128)S(1)}, f32[8,128,128]{2,1,0:T(8,128)S(1)}, /*index=5*/s32[]{:T(128)}) while((s32[]{:T(128)}, f32[8,128,128]{2,1,0:T(8,128)}, bf16[8,128,128]{2,1,0:T(8,128)(2,1)}, f32[8,128,128]{2,1,0:T(8,128)S(1)}, ...), condition=%wide.region_18.19_spmd, body=%wide.region_17.18_spmd.sunk | while | flops 201719808 | bytes 3407981 | solution.py:258
  1308.3 7.2 collective-permute-done.1
  1371.8 618.9 %while.127 = (s32[]{:T(128)}, f32[8,128,128]{2,1,0:T(8,128)S(1)}, f32[8,8,64,128]{3,1,2,0:T(8,128)}, f32[8,8,64,128]{3,1,2,0:T(8,128)}, f32[8,8,64,128]{3,1,2,0:...) while((s32[]{:T(128)}, f32[8,128,128]{2,1,0:T(8,128)S(1)}, ...), condition=%wide.region_23.24_spmd.clone, body=%wide.region_19.23_spmd.clone.sunk | while | flops 1134571520 | bytes 23290084 | solution.py:129
  1382.5 40.0 %custom-call.47 = f32[8,1,64,64]{2,3,1,0:T(8,128)} custom-call(f32[8,1,64,64]{3,2,1,0:T(8,128)S(1)} %add_bitcast_fusion.4), custom_call_target="InvertDiagBlocksLowerTriangular" | custom-call | tf_op jit(solution)/shard_map/transpose(jvp())/while/body/eval_jaxpr/triangular_solve | solution.py:109
  1459.9 40.0 %custom-call.47 = f32[8,1,64,64]{2,3,1,0:T(8,128)} custom-call(f32[8,1,64,64]{3,2,1,0:T(8,128)S(1)} %add_bitcast_fusion.4), custom_call_target="InvertDiagBlocksLowerTriangular" | custom-call | tf_op jit(solution)/shard_map/transpose(jvp())/while/body/eval_jaxpr/triangular_solve | solution.py:109
  1537.3 40.0 %custom-call.47 = f32[8,1,64,64]{2,3,1,0:T(8,128)} custom-call(f32[8,1,64,64]{3,2,1,0:T(8,128)S(1)} %add_bitcast_fusion.4), custom_call_target="InvertDiagBlocksLowerTriangular" | custom-call | tf_op jit(solution)/shard_map/transpose(jvp())/while/body/eval_jaxpr/triangular_solve | solution.py:109
  1614.6 40.0 %custom-call.47 = f32[8,1,64,64]{2,3,1,0:T(8,128)} custom-call(f32[8,1,64,64]{3,2,1,0:T(8,128)S(1)} %add_bitcast_fusion.4), custom_call_target="InvertDiagBlocksLowerTriangular" | custom-call | tf_op jit(solution)/shard_map/transpose(jvp())/while/body/eval_jaxpr/triangular_solve | solution.py:109
  1692.0 40.0 %custom-call.47 = f32[8,1,64,64]{2,3,1,0:T(8,128)} custom-call(f32[8,1,64,64]{3,2,1,0:T(8,128)S(1)} %add_bitcast_fusion.4), custom_call_target="InvertDiagBlocksLowerTriangular" | custom-call | tf_op jit(solution)/shard_map/transpose(jvp())/while/body/eval_jaxpr/triangular_solve | solution.py:109
  1769.3 40.0 %custom-call.47 = f32[8,1,64,64]{2,3,1,0:T(8,128)} custom-call(f32[8,1,64,64]{3,2,1,0:T(8,128)S(1)} %add_bitcast_fusion.4), custom_call_target="InvertDiagBlocksLowerTriangular" | custom-call | tf_op jit(solution)/shard_map/transpose(jvp())/while/body/eval_jaxpr/triangular_solve | solution.py:109
  1846.7 40.0 %custom-call.47 = f32[8,1,64,64]{2,3,1,0:T(8,128)} custom-call(f32[8,1,64,64]{3,2,1,0:T(8,128)S(1)} %add_bitcast_fusion.4), custom_call_target="InvertDiagBlocksLowerTriangular" | custom-call | tf_op jit(solution)/shard_map/transpose(jvp())/while/body/eval_jaxpr/triangular_solve | solution.py:109
  1924.0 40.0 %custom-call.47 = f32[8,1,64,64]{2,3,1,0:T(8,128)} custom-call(f32[8,1,64,64]{3,2,1,0:T(8,128)S(1)} %add_bitcast_fusion.4), custom_call_target="InvertDiagBlocksLowerTriangular" | custom-call | tf_op jit(solution)/shard_map/transpose(jvp())/while/body/eval_jaxpr/triangular_solve | solution.py:109
  2016.8 7.7 multiply_reduce_fusion.2
  2046.3 9.4 fusion.206
  2056.0 9.6 fusion.235
  2065.6 15.6 fusion.199
  2082.8 8.0 add_convert_fusion.1
  2090.8 8.0 fusion.182
  2098.8 42.1 %all-reduce.18 = (f32[1024]{0:T(1024)}, f32[4,3072]{1,0:T(4,128)}, f32[128]{0:T(128)}, f32[1024]{0:T(1024)}) all-reduce(f32[1024]{0:T(1024)S(1)} %get-tuple-element.1848, f32[4,3072]{1,0:T(4,128)S(1)} %pad_add_fusion.5, f32[128]{0:T(128)S(1)} %bitcast_reduce_fusion, ...), channel_id=1, replica_groups=mesh['dp'=4,'seq'=8] {'dp','seq'}, use_global_device_ids=true, to_apply=%region_28.29 | all-reduce | flops 14464 | bytes 115712 | tf_op jit(solution)/shard_map/psum | solution.py:289
  2145.5 126.6 %reduce-scatter.10.cloned.1.call-done = f32[32,1024]{1,0:T(8,128)} async-done(((f32[1024,1024]{1,0:T(8,128)}), f32[32,1024]{1,0:T(8,128)}) %reduce-scatter.10.cloned.1.call-update) | async-done | bytes 131088 | tf_op jit(solution)/shard_map/reduce_scatter | solution.py:279
  2272.1 160.1 %reduce-scatter.8.cloned.1.call-done = f32[32,3072]{1,0:T(8,128)} async-done(((f32[1024,3072]{1,0:T(8,128)}), f32[32,3072]{1,0:T(8,128)}) %reduce-scatter.8.cloned.1.call-update) | async-done | bytes 393232 | tf_op jit(solution)/shard_map/reduce_scatter | solution.py:273
  2432.2 163.3 %reduce-scatter.14.cloned.1.call-done = f32[88,1024]{1,0:T(8,128)} async-done(((f32[2816,1024]{1,0:T(8,128)}), f32[88,1024]{1,0:T(8,128)}) %reduce-scatter.14.cloned.1.call-update) | async-done | bytes 360464 | tf_op jit(solution)/shard_map/reduce_scatter | solution.py:286
  2595.5 253.0 %reduce-scatter.12.cloned.1.call-done = f32[32,5632]{1,0:T(8,128)} async-done(((f32[1024,5632]{1,0:T(8,128)}), f32[32,5632]{1,0:T(8,128)}) %reduce-scatter.12.cloned.1.call-update) | async-done | bytes 720912 | tf_op jit(solution)/shard_map/reduce_scatter | solution.py:282
  (1096 shorter events, 928.4 us)
Async XLA Ops:
  7.2 51.9 %copy-start.24 = (bf16[512,1024]{1,0:T(8,128)(2,1)S(1)}, bf16[512,1024]{1,0:T(8,128)(2,1)}, u32[]{:S(2)}) copy-start(bf16[512,1024]{1,0:T(8,128)(2,1)} %param.24) | copy-start | bytes 3145732
  7.2 76.2 %all-gather.6.cloned.1.call-start = ((), (), s32[]{:S(2)}) async-start(), calls=%async_computation.5 | async-start | bytes 6488064 | tf_op jit(solution)/shard_map/all_gather | solution.py:168
  7.9 1163.5 %all-gather.8.cloned.1.call-start = ((), (), s32[]{:S(2)}) async-start(), calls=%async_computation.6 | async-start | bytes 2162688 | tf_op jit(solution)/shard_map/all_gather | solution.py:170
  8.7 1167.6 %all-gather.10.cloned.1.call-start = ((), (), s32[]{:S(2)}) async-start(), calls=%async_computation.7 | async-start | bytes 11894784 | tf_op jit(solution)/shard_map/all_gather | solution.py:171
  9.4 1179.5 %all-gather.12.cloned.1.call-start = ((), (), s32[]{:S(2)}) async-start(), calls=%async_computation.8 | async-start | bytes 5947392 | tf_op jit(solution)/shard_map/all_gather | solution.py:232
  10.0 2134.1 %reduce-scatter.16.cloned.1.call-start = ((), (), s32[]{:S(2)}) async-start(), calls=%async_computation.13 | async-start | bytes 540672
  11.1 83.6 %copy-start.47 = (f32[512]{0:T(512)}, f32[512]{0:T(512)S(1)}, u32[]{:S(2)}) copy-start(f32[512]{0:T(512)S(1)} %get-tuple-element.2078) | copy-start | bytes 6148
  11.1 83.7 %copy-start.49 = (f32[512]{0:T(512)}, f32[512]{0:T(512)S(1)}, u32[]{:S(2)}) copy-start(f32[512]{0:T(512)S(1)} %get-tuple-element.2079) | copy-start | bytes 6148
  11.2 83.7 %copy-start.51 = (f32[512]{0:T(512)}, f32[512]{0:T(512)S(1)}, u32[]{:S(2)}) copy-start(f32[512]{0:T(512)S(1)} %get-tuple-element.2080) | copy-start | bytes 6148
  12.6 70.8 %copy-start.55 = (f32[1024]{0:T(1024)}, f32[1024]{0:T(1024)S(1)}, u32[]{:S(2)}) copy-start(f32[1024]{0:T(1024)S(1)} %convert_element_type.213) | copy-start | bytes 12292
  14.1 69.3 %copy-start.57 = (f32[512]{0:T(512)}, f32[512]{0:T(512)S(1)}, u32[]{:S(2)}) copy-start(f32[512]{0:T(512)S(1)} %fusion.215) | copy-start | bytes 6148
  15.1 79.8 %copy-start.35 = (f32[1,3072]{1,0:T(1,128)}, f32[1,3072]{1,0:T(1,128)S(1)}, u32[]{:S(2)}) copy-start(f32[1,3072]{1,0:T(1,128)S(1)} %get-tuple-element.2072) | copy-start | bytes 36868
  15.1 79.8 %copy-start.37 = (f32[1,3072]{1,0:T(1,128)}, f32[1,3072]{1,0:T(1,128)S(1)}, u32[]{:S(2)}) copy-start(f32[1,3072]{1,0:T(1,128)S(1)} %get-tuple-element.2073) | copy-start | bytes 36868
  15.1 79.8 %copy-start.39 = (f32[1,3072]{1,0:T(1,128)}, f32[1,3072]{1,0:T(1,128)S(1)}, u32[]{:S(2)}) copy-start(f32[1,3072]{1,0:T(1,128)S(1)} %get-tuple-element.2074) | copy-start | bytes 36868
  15.1 79.8 %copy-start.41 = (f32[1,3072]{1,0:T(1,128)}, f32[1,3072]{1,0:T(1,128)S(1)}, u32[]{:S(2)}) copy-start(f32[1,3072]{1,0:T(1,128)S(1)} %get-tuple-element.2075) | copy-start | bytes 36868
  59.5 34.9 %copy-start.61 = (bf16[1024]{0:T(1024)(128)(2,1)S(1)}, bf16[1024]{0:T(1024)(128)(2,1)}, u32[]{:S(2)}) copy-start(bf16[1024]{0:T(1024)(128)(2,1)} %param.32) | copy-start | bytes 6148
  91.8 3.0 collective-permute-start.2
  561.8 4.7 collective-permute-start
  568.4 7.8 collective-permute-start
  578.2 7.9 collective-permute-start
  588.0 7.9 collective-permute-start
  597.8 7.9 collective-permute-start
  607.7 7.9 collective-permute-start
  617.5 7.9 collective-permute-start
  637.9 45.5 %copy-start = (f32[8,128,128]{2,1,0:T(8,128)S(1)}, f32[8,128,128]{2,1,0:T(8,128)}, u32[]{:S(2)}) copy-start(f32[8,128,128]{2,1,0:T(8,128)} %get-tuple-element.2718) | copy-start | bytes 1572868 | tf_op jit(solution)/shard_map/jvp()/while
  704.7 45.4 %copy-start = (f32[8,128,128]{2,1,0:T(8,128)S(1)}, f32[8,128,128]{2,1,0:T(8,128)}, u32[]{:S(2)}) copy-start(f32[8,128,128]{2,1,0:T(8,128)} %get-tuple-element.2718) | copy-start | bytes 1572868 | tf_op jit(solution)/shard_map/jvp()/while
  771.4 45.5 %copy-start = (f32[8,128,128]{2,1,0:T(8,128)S(1)}, f32[8,128,128]{2,1,0:T(8,128)}, u32[]{:S(2)}) copy-start(f32[8,128,128]{2,1,0:T(8,128)} %get-tuple-element.2718) | copy-start | bytes 1572868 | tf_op jit(solution)/shard_map/jvp()/while
  838.2 45.4 %copy-start = (f32[8,128,128]{2,1,0:T(8,128)S(1)}, f32[8,128,128]{2,1,0:T(8,128)}, u32[]{:S(2)}) copy-start(f32[8,128,128]{2,1,0:T(8,128)} %get-tuple-element.2718) | copy-start | bytes 1572868 | tf_op jit(solution)/shard_map/jvp()/while
  904.9 45.5 %copy-start = (f32[8,128,128]{2,1,0:T(8,128)S(1)}, f32[8,128,128]{2,1,0:T(8,128)}, u32[]{:S(2)}) copy-start(f32[8,128,128]{2,1,0:T(8,128)} %get-tuple-element.2718) | copy-start | bytes 1572868 | tf_op jit(solution)/shard_map/jvp()/while
  971.6 45.4 %copy-start = (f32[8,128,128]{2,1,0:T(8,128)S(1)}, f32[8,128,128]{2,1,0:T(8,128)}, u32[]{:S(2)}) copy-start(f32[8,128,128]{2,1,0:T(8,128)} %get-tuple-element.2718) | copy-start | bytes 1572868 | tf_op jit(solution)/shard_map/jvp()/while
  1038.3 45.4 %copy-start = (f32[8,128,128]{2,1,0:T(8,128)S(1)}, f32[8,128,128]{2,1,0:T(8,128)}, u32[]{:S(2)}) copy-start(f32[8,128,128]{2,1,0:T(8,128)} %get-tuple-element.2718) | copy-start | bytes 1572868 | tf_op jit(solution)/shard_map/jvp()/while
  1105.0 45.4 %copy-start = (f32[8,128,128]{2,1,0:T(8,128)S(1)}, f32[8,128,128]{2,1,0:T(8,128)}, u32[]{:S(2)}) copy-start(f32[8,128,128]{2,1,0:T(8,128)} %get-tuple-element.2718) | copy-start | bytes 1572868 | tf_op jit(solution)/shard_map/jvp()/while
  1297.3 7.8 collective-permute-start.1
  1307.1 8.5 collective-permute-start.1
  1317.5 7.9 collective-permute-start.1
  1327.4 7.9 collective-permute-start.1
  1337.2 7.9 collective-permute-start.1
  1347.0 7.9 collective-permute-start.1
  1356.8 7.9 collective-permute-start.1
  1371.8 619.9 %copy-start.46 = (f32[512,8]{0,1:T(8,128)S(1)}, f32[512,8]{0,1:T(8,128)}, u32[]{:S(2)}) copy-start(f32[512,8]{0,1:T(8,128)} %copy-done.45) | copy-start | bytes 49156
  1371.8 619.9 %copy-start.56 = (f32[1024]{0:T(1024)S(1)}, f32[1024]{0:T(1024)}, u32[]{:S(2)}) copy-start(f32[1024]{0:T(1024)} %copy-done.55) | copy-start | bytes 12292
  1371.8 619.9 %copy-start.58 = (f32[512]{0:T(512)S(1)}, f32[512]{0:T(512)}, u32[]{:S(2)}) copy-start(f32[512]{0:T(512)} %copy-done.57) | copy-start | bytes 6148
  1994.5 277.7 %reduce-scatter.10.cloned.1.call-start = ((), (), s32[]{:S(2)}) async-start(), calls=%async_computation.10 | async-start | bytes 4325376 | tf_op jit(solution)/shard_map/reduce_scatter | solution.py:279
  1999.4 432.8 %reduce-scatter.8.cloned.1.call-start = ((), (), s32[]{:S(2)}) async-start(), calls=%async_computation.9 | async-start | bytes 12976128 | tf_op jit(solution)/shard_map/reduce_scatter | solution.py:273
  2038.9 7.4 collective-permute-start.3
  2055.7 539.8 %reduce-scatter.14.cloned.1.call-start = ((), (), s32[]{:S(2)}) async-start(), calls=%async_computation.12 | async-start | bytes 11894784 | tf_op jit(solution)/shard_map/reduce_scatter | solution.py:286
  2065.6 782.9 %reduce-scatter.12.cloned.1.call-start = ((), (), s32[]{:S(2)}) async-start(), calls=%async_computation.11 | async-start | bytes 23789568 | tf_op jit(solution)/shard_map/reduce_scatter | solution.py:282
  2090.8 50.2 %copy-start.54 = (f32[512]{0:T(512)S(1)}, f32[512]{0:T(512)}, u32[]{:S(2)}) copy-start(f32[512]{0:T(512)} %copy-done.53) | copy-start | bytes 6148
  (87 other events, 469.8 us)
Sparse Core Ops, SparseCore 0:
  11.0 72.3 all-gather.5
  86.4 55.1 all-gather.7
  144.5 91.5 all-gather.9
  238.8 67.1 all-gather.11
  1994.6 135.9 reduce-scatter.15
  2133.4 138.6 reduce-scatter.9
  2279.7 152.4 reduce-scatter.7
  2435.1 160.3 reduce-scatter.13
  2598.4 250.0 reduce-scatter.11
where the time goes:
time: 2870 us; the launch traced here: 2860 us
  other arithmetic  1160 us (40%)
  waiting for transfers between devices  792 us (28%)
  matrix products  534 us (19%)
  local copies, waits for them, and re-layouts  202 us (7%)
  blocking collectives  85.9 us (3%)
  starting transfers between devices  55.8 us (2%)
    another operation x96, other arithmetic, advance(): lax.linalg.triangular_solve(lower_mat, right_side, left_side=True, lower=...  987 us
    reduce_scatter x1, waiting for transfers between devices, local(): lax.psum_scatter(contract_rows(xn2, d_gate_up), ('dp', 'seq'), scatter_di...  253 us
    reduce_scatter x1, waiting for transfers between devices, local(): lax.psum_scatter(contract_rows(hidden, grad_out), ('dp', 'seq'), scatter_...  163 us
    reduce_scatter x1, waiting for transfers between devices, local(): lax.psum_scatter(contract_rows(xn1, d_proj_b), ('dp', 'seq'), scatter_dim...  160 us
    reduce_scatter x1, waiting for transfers between devices, local(): lax.psum_scatter(contract_rows(head_out, d_att), ('dp', 'seq'), scatter_d...  127 us
    dot_general x32, matrix products, advance(): jnp.einsum('hck,hrk->hcr', query_block, carried, precision=highest)  75.5 us
    dot_general x40, matrix products, advance(): jnp.einsum('hck,hrk->hcr', solved[..., extent:], carried, precision=highest)  75.4 us
    dynamic_slice x72, local copies, waits for them, and re-layouts, delta_pass(): ending, results = lax.scan(advance, state, pieces)  72.5 us
  transfers between devices with their start and end apart: 25, of which 21 were waited for; matrix products, arithmetic and copies ran while one was open for 40% of the time, Pallas kernels for 0%

commit v1 on v0

v1 whole, which is shorter than its diff:
```python
import functools

import jax
import jax.numpy as jnp
from jax import lax
from jax.experimental import pallas as pl
from jax.experimental.pallas import tpu as pltpu
from jax.sharding import PartitionSpec as P

norm_eps = 1e-05
unit_eps = 1e-06
MESH = pl.DeviceIdType.MESH
f32, bf16 = jnp.float32, jnp.bfloat16
HIGH = lax.Precision.HIGH
VMEM_LIMIT = 56 << 20


def nn(a, b, prec=None):
    return lax.dot_general(a, b, (((1,), (0,)), ((), ())), precision=prec, preferred_element_type=f32)


def nt(a, b, prec=None):
    return lax.dot_general(a, b, (((1,), (1,)), ((), ())), precision=prec, preferred_element_type=f32)


def tn(a, b, prec=None):
    return lax.dot_general(a, b, (((0,), (0,)), ((), ())), precision=prec, preferred_element_type=f32)


def unit_lower_inverse(a, row, col):
    size = a.shape[0]
    block = min(8, size)
    eye = (row == col).astype(f32)
    step = jnp.where(row // block == col // block, -a, 0.0)
    inverse = eye + step
    power = block // 2
    while power >= 1:
        if power > 0 and block > 2:
            step = nn(step, step, HIGH)
            inverse = inverse + nn(inverse, step, HIGH)
        power //= 2
        if power < 2:
            break
    while block < size:
        off = jnp.where((row // (2 * block) == col // (2 * block)) & (row // block == col // block + 1), a, 0.0)
        inverse = inverse - nn(inverse, nn(off, inverse, HIGH), HIGH)
        block *= 2
    return inverse


def head_column(matrix, head):
    lane = lax.broadcasted_iota(jnp.int32, matrix.shape, 1)
    return jnp.sum(jnp.where(lane == head, matrix, 0.0), axis=1, keepdims=True)


def masks_of(docs_col, docs_row):
    size = docs_col.shape[0]
    row = lax.broadcasted_iota(jnp.int32, (size, size), 0)
    col = lax.broadcasted_iota(jnp.int32, (size, size), 1)
    same = docs_col == docs_row
    return row, col, same


def local_kernel(
    chunk, pq, pk, pv, hq, hk, hv, tq, tk, tv, aux, docs_c, docs_r, logits,
    cq, ck, cv, w_o, u_o, qt_o, o_o, t_o, p_o, kk_o, dt_o, ft_o, seg_o, pad,
):
    head = pl.program_id(0)
    rows, width = pq.shape
    keeps = (aux[:, 2:3], aux[:, 3:4], aux[:, 4:5])
    acts = []
    for src, halo, taps, dst in ((pq, hq, tq, cq), (pk, hk, tk, ck), (pv, hv, tv, cv)):
        pad[0:8, :] = halo[...]
        pad[8 : 8 + rows, :] = src[...]
        conv = taps[3:4, :] * src[...]
        for back in (1, 2, 3):
            conv = conv + taps[3 - back : 4 - back, :] * (pad[8 - back : 8 - back + rows, :] * keeps[back - 1])
        dst[...] = conv
        acts.append(conv * jax.nn.sigmoid(conv))
    q = acts[0] * (lax.rsqrt(jnp.sum(acts[0] * acts[0], axis=1, keepdims=True) + unit_eps) * width ** (-0.5))
    k = acts[1] * lax.rsqrt(jnp.sum(acts[1] * acts[1], axis=1, keepdims=True) + unit_eps)
    v = acts[2]
    beta = jax.nn.sigmoid(head_column(logits[...], head))
    cont, last = aux[:, 0:1], aux[:, 1:2]
    seg = None
    for c in range(rows // chunk):
        sl = slice(c * chunk, (c + 1) * chunk)
        row, col, same = masks_of(docs_c[sl, :], docs_r[:, sl])
        qc, kc, vc, bc, cc, lc = q[sl], k[sl], v[sl], beta[sl], cont[sl], last[sl]
        kk = nt(kc, kc, HIGH)
        a = jnp.where(same & (row > col), bc * kk, 0.0)
        t = unit_lower_inverse(a, row, col)
        wu = nn(t, jnp.concatenate([(bc * cc) * kc, bc * vc], axis=1), HIGH)
        p = jnp.where(same & (row >= col), nt(qc, kc, HIGH), 0.0)
        pwu = nn(p, wu, HIGH)
        x = tn(lc * kc, wu, HIGH)
        d_row = lax.broadcasted_iota(jnp.int32, (width, width), 0)
        d_col = lax.broadcasted_iota(jnp.int32, (width, width), 1)
        dt = jnp.where(d_row == d_col, cc[chunk - 1 : chunk], 0.0) - x[:, :width]
        ft = x[:, width:]
        w_o[sl, :] = wu[:, :width]
        u_o[sl, :] = wu[:, width:]
        qt_o[sl, :] = cc * qc - pwu[:, :width]
        o_o[sl, :] = pwu[:, width:]
        t_o[sl, :] = t
        p_o[sl, :] = p
        kk_o[sl, :] = kk
        dt_o[c * width : (c + 1) * width, :] = dt
        ft_o[c * width : (c + 1) * width, :] = ft
        if seg is None:
            seg = jnp.concatenate([dt, ft], axis=1)
        else:
            seg = nn(dt, seg, HIGH)
            seg = jnp.concatenate([seg[:, :width], seg[:, width:] + ft], axis=1)
    seg_o[...] = seg


def relay_kernel(n_seq, back, map_ref, add_ref, out_ref, send, ssem, rsem):
    d, s = lax.axis_index("dp"), lax.axis_index("seq")
    heads = map_ref.shape[0]
    if back:
        first, final = s == n_seq - 1, s == 0
        ahead, behind = s - 1, s + 1
    else:
        first, final = s == 0, s == n_seq - 1
        ahead, behind = s + 1, s - 1
    barrier = pltpu.get_barrier_semaphore()

    @pl.when(jnp.logical_not(first))
    def _():
        pl.semaphore_signal(barrier, inc=1, device_id=(d, behind), device_id_type=MESH)

    @pl.when(jnp.logical_not(final))
    def _():
        pl.semaphore_signal(barrier, inc=1, device_id=(d, ahead), device_id_type=MESH)

    pl.semaphore_wait(barrier, jnp.where(first | final, 1, 2))

    def copy_of(h):
        return pltpu.make_async_remote_copy(
            src_ref=send.at[h], dst_ref=out_ref.at[h], send_sem=ssem.at[h], recv_sem=rsem.at[h],
            device_id=(d, ahead), device_id_type=MESH,
        )

    @pl.when(first)
    def _():
        out_ref[...] = jnp.zeros(out_ref.shape, out_ref.dtype)

    for h in range(heads):
        @pl.when(jnp.logical_not(first))
        def _():
            copy_of(h).wait_recv()

        @pl.when(jnp.logical_not(final))
        def _():
            state = out_ref[h].astype(f32)
            mult = tn if back else nn
            send[h] = (mult(map_ref[h], state, HIGH) + add_ref[h]).astype(bf16)
            copy_of(h).start()

    @pl.when(jnp.logical_not(final))
    def _():
        for h in range(heads):
            copy_of(h).wait_send()


def output_kernel(chunk, zin, dt, ft, qt, o0, gain, z_o, o_o, head_o):
    rows, width = qt.shape
    z = zin[0].astype(f32)
    for c in range(rows // chunk):
        sl = slice(c * chunk, (c + 1) * chunk)
        ds = slice(c * width, (c + 1) * width)
        z_o[ds, :] = z
        o = o0[sl, :] + nn(qt[sl, :], z, HIGH)
        o_o[sl, :] = o
        scale = lax.rsqrt(jnp.mean(o * o, axis=1, keepdims=True) + norm_eps)
        head_o[sl, :] = (o * scale * gain[...]).astype(bf16)
        if c + 1 < rows // chunk:
            z = nn(dt[ds, :], z, HIGH) + ft[ds, :]


def seed_kernel(chunk, dh, o, gain, qt, dt, do_o, b_o, seed_o, dgain_o):
    head = pl.program_id(0)
    rows, width = qt.shape
    ov, dhv = o[...], dh[...]
    scale = lax.rsqrt(jnp.mean(ov * ov, axis=1, keepdims=True) + norm_eps)
    n = ov * scale
    dg = jnp.sum(dhv * n, axis=0, keepdims=True)
    dgain_o[...] = jnp.where(head == 0, 0.0, dgain_o[...]) + jnp.broadcast_to(dg, dgain_o.shape)
    y = dhv * gain[...]
    do = (y - n * jnp.mean(y * n, axis=1, keepdims=True)) * scale
    do_o[...] = do
    g = None
    for c in reversed(range(rows // chunk)):
        sl = slice(c * chunk, (c + 1) * chunk)
        ds = slice(c * width, (c + 1) * width)
        b_o[ds, :] = tn(qt[sl, :], do[sl], HIGH)
        g = b_o[ds, :] if g is None else tn(dt[ds, :], g, HIGH) + b_o[ds, :]
    seed_o[0] = g


def back_kernel(
    chunk, pq, pk, pv, hq, hk, hv, tq, tk, tv, aux, docs_c, docs_r, logits,
    cq, ck, cv, w_r, u_r, t_r, p_r, kk_r, z_r, do_r, dt_r, b_r, g_r,
    dpq, dpk, dpv, dhq, dhk, dhv, dtq, dtk, dtv, dlogit_o, pad, mask1, mask2, mask3,
):
    head = pl.program_id(0)
    rows, width = pq.shape
    cont, last = aux[:, 0:1], aux[:, 1:2]
    keeps = (aux[:, 2:3], aux[:, 3:4], aux[:, 4:5])
    scale = width ** (-0.5)
    beta = jax.nn.sigmoid(head_column(logits[...], head))
    sq, sk, sv = (jax.nn.sigmoid(x[...]) for x in (cq, ck, cv))
    aq, ak, v = cq[...] * sq, ck[...] * sk, cv[...] * sv
    iq = lax.rsqrt(jnp.sum(aq * aq, axis=1, keepdims=True) + unit_eps)
    ik = lax.rsqrt(jnp.sum(ak * ak, axis=1, keepdims=True) + unit_eps)
    uq, k = aq * iq, ak * ik
    q = uq * scale
    g = g_r[0].astype(f32)
    dqs, dks, dvs, dbs = [], [], [], []
    for c in reversed(range(rows // chunk)):
        sl = slice(c * chunk, (c + 1) * chunk)
        ds = slice(c * width, (c + 1) * width)
        row, col, same = masks_of(docs_c[sl, :], docs_r[:, sl])
        qc, kc, vc, bc, cc, lc = q[sl], k[sl], v[sl], beta[sl], cont[sl], last[sl]
        z = z_r[ds, :]
        do = do_r[sl, :]
        wkz = nn(jnp.concatenate([w_r[sl, :], kc], axis=0), z)
        u = u_r[sl, :] - wkz[:chunk]
        kz = wkz[chunk:]
        du = tn(p_r[sl, :], do) + nn(lc * kc, g)
        dr = tn(t_r[sl, :], du)
        y = nt(jnp.concatenate([do, dr], axis=0), jnp.concatenate([u, z], axis=0))
        dp = jnp.where(same & (row >= col), y[:chunk, :chunk], 0.0)
        da = jnp.where(same & (row > col), -y[chunk:, :chunk], 0.0)
        bda = bc * da
        pak = nn(jnp.concatenate([dp, bda], axis=0), kc)
        dqs.append(cc * y[:chunk, chunk:] + pak[:chunk])
        dks.append(
            tn(jnp.concatenate([dp, bda], axis=0), jnp.concatenate([qc, kc], axis=0))
            + pak[chunk:] + lc * nt(u, g) - (bc * cc) * y[chunk:, chunk:]
        )
        dvs.append(bc * dr)
        dbs.append(
            jnp.sum(dr * (vc - cc * kz), axis=1, keepdims=True)
            + jnp.sum(da * kk_r[sl, :], axis=1, keepdims=True)
        )
        if c > 0:
            g = tn(dt_r[ds, :], g) + b_r[ds, :]
    dq, dk, dv, db = (jnp.concatenate(x[::-1], axis=0) for x in (dqs, dks, dvs, dbs))
    lane = lax.broadcasted_iota(jnp.int32, dlogit_o.shape, 1)
    dlogit_o[...] = jnp.where(lane == head, db * beta * (1.0 - beta), jnp.where(head == 0, 0.0, dlogit_o[...]))
    du_q = dq * scale
    da_q = (du_q - uq * jnp.sum(uq * du_q, axis=1, keepdims=True)) * iq
    da_k = (dk - k * jnp.sum(k * dk, axis=1, keepdims=True)) * ik
    for dact, sg, c_r, src, halo, taps, dst, dhalo, dtaps in (
        (da_q, sq, cq, pq, hq, tq, dpq, dhq, dtq),
        (da_k, sk, ck, pk, hk, tk, dpk, dhk, dtk),
        (dv, sv, cv, pv, hv, tv, dpv, dhv, dtv),
    ):
        dconv = dact * (sg * (1.0 + c_r[...] * (1.0 - sg)))
        pad[0:8, :] = halo[...]
        pad[8 : 8 + rows, :] = src[...]
        zero = jnp.zeros((8, width), f32)
        total = taps[3:4, :] * dconv
        early = zero
        gtaps = [None] * 4
        gtaps[3] = jnp.sum(dconv * src[...], axis=0, keepdims=True)
        for back, mask in ((1, mask1), (2, mask2), (3, mask3)):
            kept = dconv * keeps[back - 1]
            gtaps[3 - back] = jnp.sum(kept * pad[8 - back : 8 - back + rows, :], axis=0, keepdims=True)
            mask[0:8, :] = zero
            mask[8 : 8 + rows, :] = kept
            mask[8 + rows : 16 + rows, :] = zero
            total = total + taps[3 - back : 4 - back, :] * mask[8 + back : 8 + back + rows, :]
            early = early + taps[3 - back : 4 - back, :] * mask[back : back + 8, :]
        dst[...] = total
        dhalo[...] = early
        dtaps[...] = jnp.concatenate(gtaps + [jnp.zeros((4, width), f32)], axis=0)


def from_behind(value, axis, steps):
    count = lax.axis_size(axis)
    first, last = (max(0, -steps), min(count, count - steps))
    return lax.ppermute(value, axis, [(source, source + steps) for source in range(first, last)])


def rms_scale(values, gain):
    return values * lax.rsqrt(jnp.mean(values * values, axis=-1, keepdims=True) + norm_eps) * gain


def doc_ids(lengths, positions):
    ends = jnp.cumsum(lengths)
    inside = (positions[:, None] >= ends[None, :]).astype(jnp.int32)
    return jnp.where(positions >= 0, jnp.sum(inside, axis=1), -1)


def swiglu(gate_up):
    half = gate_up.shape[1] // 2
    return jax.nn.silu(gate_up[:, :half]) * gate_up[:, half:]


def contract_rows(left, right):
    return tn(left, right)


def contract_cols(left, right):
    return nt(left, right)


def local(
    n_seq, tokens, doc_lengths, norm_gain, w_qkv, w_beta, conv_weight, head_gain, w_out, mlp_gain, w_mlp_in, w_down, grad_out,
):
    rows, model = tokens.shape
    heads = w_beta.shape[1]
    width = head_gain.shape[0]
    taps_n = conv_weight.shape[0]
    qkv = w_qkv.shape[1]
    chunk = min(128, rows)
    n_chunk = rows // chunk
    both = ("dp", "seq")

    w_in = lax.all_gather(
        jnp.concatenate([w_qkv, jnp.pad(w_beta, ((0, 0), (0, 128 - heads)))], axis=1), both, axis=0, tiled=True
    )
    w_o = lax.all_gather(w_out, both, axis=0, tiled=True)
    w_m = lax.all_gather(w_mlp_in, both, axis=0, tiled=True)
    w_d = lax.all_gather(w_down, both, axis=0, tiled=True)

    inputs = tokens.astype(f32)
    norm_one, pull_one = jax.vjp(rms_scale, inputs, norm_gain.astype(f32))
    xn1 = norm_one.astype(bf16)
    projected = nn(xn1, w_in)
    logits = projected[:, qkv : qkv + heads]
    start = lax.axis_index("seq") * rows
    docs_pad = doc_ids(doc_lengths[0], start - taps_n + 1 + jnp.arange(rows + taps_n - 1, dtype=jnp.int32))
    docs = docs_pad[taps_n - 1 :]
    by_chunk = docs.reshape(n_chunk, chunk)
    before = docs_pad[taps_n - 2 : taps_n - 2 + rows].reshape(n_chunk, chunk)[:, :1]
    aux = jnp.stack(
        [(by_chunk == before).reshape(-1), (by_chunk == by_chunk[:, -1:]).reshape(-1)]
        + [docs_pad[taps_n - 1 - b : taps_n - 1 - b + rows] == docs for b in (1, 2, 3)]
        + [docs < -5] * 3,
        axis=1,
    ).astype(f32)
    docs_c, docs_r = docs[:, None], docs[None, :]
    received = from_behind(projected[rows - taps_n + 1 :, :qkv].astype(bf16), "seq", 1).astype(f32)
    halo = jnp.pad(received, ((8 - taps_n + 1, 0), (0, 0)))
    taps = jnp.pad(conv_weight.astype(f32), ((0, 8 - taps_n), (0, 0)))

    def third(block_rows):
        return [pl.BlockSpec((block_rows, width), lambda h, t=t: (0, t * heads + h)) for t in range(3)]

    def per_head(block_rows):
        return pl.BlockSpec((block_rows, width), lambda h: (0, h))

    def whole(shape):
        return pl.BlockSpec(shape, lambda h: (0,) * len(shape))

    state_block = pl.BlockSpec((1, width, width), lambda h: (h, 0, 0))
    params = pltpu.CompilerParams(vmem_limit_bytes=VMEM_LIMIT, dimension_semantics=("arbitrary",))
    cols = heads * width
    token_like = jax.ShapeDtypeStruct((rows, cols), f32)
    chunk_like = jax.ShapeDtypeStruct((rows, heads * chunk), f32)
    state_like = jax.ShapeDtypeStruct((n_chunk * width, cols), f32)
    common_specs = (
        third(rows) + third(8) + third(8)
        + [whole((rows, 8)), whole((rows, 1)), whole((1, rows)), whole((rows, heads))]
    )
    common = (projected,) * 3 + (halo,) * 3 + (taps,) * 3 + (aux, docs_c, docs_r, logits)
    chunk_block = pl.BlockSpec((rows, chunk), lambda h: (0, h))
    cq, ck, cv, w_s, u_s, qt, o0, t_s, p_s, kk_s, dt, ft, seg = pl.pallas_call(
        functools.partial(local_kernel, chunk),
        grid=(heads,),
        in_specs=common_specs,
        out_specs=[per_head(rows)] * 7 + [chunk_block] * 3 + [per_head(n_chunk * width)] * 2
        + [pl.BlockSpec((width, 2 * width), lambda h: (0, h))],
        out_shape=[token_like] * 7 + [chunk_like] * 3 + [state_like] * 2
        + [jax.ShapeDtypeStruct((width, 2 * cols), f32)],
        scratch_shapes=[pltpu.VMEM((rows + 8, width), f32)],
        compiler_params=params,
        name="delta_local",
    )(*common)
    seg = seg.reshape(width, heads, 2, width)
    seg_map, seg_add = (jnp.swapaxes(seg[:, :, i], 0, 1) for i in (0, 1))

    def relay(back, maps, adds, cid):
        return pl.pallas_call(
            functools.partial(relay_kernel, n_seq, back),
            in_specs=[pl.BlockSpec(memory_space=pltpu.VMEM)] * 2,
            out_specs=pl.BlockSpec(memory_space=pltpu.VMEM),
            out_shape=jax.ShapeDtypeStruct((heads, width, width), bf16),
            scratch_shapes=[
                pltpu.VMEM((heads, width, width), bf16),
                pltpu.SemaphoreType.DMA((heads,)),
                pltpu.SemaphoreType.DMA((heads,)),
            ],
            compiler_params=pltpu.CompilerParams(collective_id=cid, has_side_effects=True, vmem_limit_bytes=VMEM_LIMIT),
            name="relay_back" if back else "relay",
        )(maps, adds)

    state_in = relay(False, seg_map, seg_add, 0)
    gain_h = head_gain.astype(f32)[None, :]
    z_s, mixed, head_out = pl.pallas_call(
        functools.partial(output_kernel, chunk),
        grid=(heads,),
        in_specs=[state_block, per_head(n_chunk * width), per_head(n_chunk * width), per_head(rows), per_head(rows), whole((1, width))],
        out_specs=[per_head(n_chunk * width), per_head(rows), per_head(rows)],
        out_shape=[state_like, token_like, jax.ShapeDtypeStruct((rows, cols), bf16)],
        compiler_params=params,
        name="delta_out",
    )(state_in, dt, ft, qt, o0, gain_h)

    hidden_one = inputs + nn(head_out, w_o)
    norm_two, pull_two = jax.vjp(rms_scale, hidden_one, mlp_gain.astype(f32))
    xn2 = norm_two.astype(bf16)
    gate_up = nn(xn2, w_m)
    hidden_f, pull_act = jax.vjp(swiglu, gate_up)
    hidden = hidden_f.astype(bf16)
    out = (hidden_one + nn(hidden, w_d)).astype(bf16)

    grad_in = grad_out.astype(f32)
    d_hidden = contract_cols(grad_out, w_d)
    d_gate_up = pull_act(d_hidden)[0].astype(bf16)
    d_from_two, d_mlp_gain = pull_two(contract_cols(d_gate_up, w_m))
    d_hidden_one = grad_in + d_from_two
    d_att = d_hidden_one.astype(bf16)
    d_head = contract_cols(d_att, w_o)

    do, b_s, seed, d_head_gain = pl.pallas_call(
        functools.partial(seed_kernel, chunk),
        grid=(heads,),
        in_specs=[per_head(rows), per_head(rows), whole((1, width)), per_head(rows), per_head(n_chunk * width)],
        out_specs=[per_head(rows), per_head(n_chunk * width), state_block, whole((8, width))],
        out_shape=[token_like, state_like, jax.ShapeDtypeStruct((heads, width, width), f32), jax.ShapeDtypeStruct((8, width), f32)],
        compiler_params=params,
        name="delta_seed",
    )(d_head, mixed, gain_h, qt, dt)
    grad_end = relay(True, seg_map, seed, 1)
    outs = pl.pallas_call(
        functools.partial(back_kernel, chunk),
        grid=(heads,),
        in_specs=common_specs + [per_head(rows)] * 5 + [chunk_block] * 3
        + [per_head(n_chunk * width), per_head(rows), per_head(n_chunk * width), per_head(n_chunk * width), state_block],
        out_specs=[per_head(rows)] * 3 + [per_head(8)] * 6 + [whole((rows, heads))],
        out_shape=[token_like] * 3 + [jax.ShapeDtypeStruct((8, cols), f32)] * 6 + [jax.ShapeDtypeStruct((rows, heads), f32)],
        scratch_shapes=[pltpu.VMEM((rows + 8, width), f32)] + [pltpu.VMEM((rows + 16, width), f32)] * 3,
        compiler_params=params,
        name="delta_back",
    )(*common, cq, ck, cv, w_s, u_s, t_s, p_s, kk_s, z_s, do, dt, b_s, grad_end)
    d_main = jnp.concatenate(outs[:3], axis=1)
    d_early = jnp.concatenate(outs[3:6], axis=1)
    d_conv = jnp.concatenate(outs[6:9], axis=1)[:taps_n]
    d_logits = outs[9]
    returned = from_behind(d_early[8 - taps_n + 1 :].astype(bf16), "seq", -1).astype(f32)
    d_projected = d_main + jnp.pad(returned, ((rows - taps_n + 1, 0), (0, 0)))
    d_proj_b = jnp.concatenate(
        [d_projected.astype(bf16), jnp.pad(d_logits.astype(bf16), ((0, 0), (0, 128 - heads)))], axis=1
    )
    d_from_one, d_norm_gain = pull_one(contract_cols(d_proj_b, w_in))
    grad_tokens = (d_hidden_one + d_from_one).astype(bf16)

    def scatter(grad):
        return lax.psum_scatter(grad.astype(bf16), both, scatter_dimension=0, tiled=True).astype(f32)

    g_down = scatter(contract_rows(hidden, grad_out))
    g_mlp = scatter(contract_rows(xn2, d_gate_up))
    g_out = scatter(contract_rows(head_out, d_att))
    g_in = scatter(contract_rows(xn1, d_proj_b))
    small = lax.psum((d_norm_gain, d_conv, d_head_gain[0], d_mlp_gain), both)
    return (
        out, grad_tokens, small[0], g_in[:, :qkv], g_in[:, qkv : qkv + heads], small[1], small[2], g_out, small[3], g_mlp, g_down,
    )


def solution(mesh):
    split = P(("dp", "seq"), None)
    placed = (split, P("dp", None), P(), split, split, P(), P(), split, P(), split, split, split)
    return jax.shard_map(
        functools.partial(local, mesh.shape["seq"]),
        mesh=mesh,
        in_specs=placed,
        out_specs=(split, split, P(), split, split, P(), P(), split, P(), split, split),
        check_vma=False,
    )
```

time: 2870 us -> 947 us (0.33)
  other arithmetic: 1160 us -> 26.5 us
  matrix products: 534 us -> 100 us
  waiting for transfers between devices: 792 us -> 571 us
  local copies, waits for them, and re-layouts: 202 us -> 15.6 us
  Pallas kernels: 0 us -> 164 us
  starting transfers between devices: 55.8 us -> 4.25 us
  blocking collectives: 85.9 us -> 42 us
    another operation x111 -> x4, other arithmetic: 988 us -> 3.11 us  [the longest x96 987 us: advance(): lax.linalg.triangular_solve(lower_mat, right_side, left_side=True, lower=...]
    dot_general x236 -> x12, matrix products: 471 us -> 100 us  [the longest x4 38.7 us: nt(): lax.dot_general(a, b, (((1,), (1,)), ((), ())), precision=prec, preferred...]
    reduce_scatter x4, waiting for transfers between devices: 703 us -> 417 us  [scatter(): lax.psum_scatter(grad.astype(bf16), both, scatter_dimension=0, tiled=True)]
    pallas_call x0 -> x6, Pallas kernels: none -> 164 us  [the longest x1 86.5 us: local(): pl.pallas_call(functools.partial(local_kernel, chunk), grid=(heads,), in_...]
    all_gather x4, waiting for transfers between devices: 23.9 us -> 151 us  [the longest x1 68.3 us: local(): lax.all_gather(jnp.concatenate([w_qkv, jnp.pad(w_beta, ((0, 0), (0, 128 -...]
    dynamic_slice x72 -> x0, local copies, waits for them, and re-layouts: 72.5 us -> none  [delta_pass(): ending, results = lax.scan(advance, state, pieces)]
    ppermute x16 -> x2, waiting for transfers between devices: 62.4 us -> 0.82 us  [from_behind(): lax.ppermute(value, axis, [(source, source + steps) for source in range(f...]
    another operation x32 -> x0, matrix products: 60.5 us -> none  [advance(): lax.linalg.triangular_solve(lower_mat, right_side, left_side=True, lower=...]
  transfers between devices with their start and end apart: 25 -> 10, of which waited for: 21 -> 7; matrix products, arithmetic and copies ran while one was open for 40% -> 11% of each run, Pallas kernels for 0% -> 17%
where the time goes in v1:
time: 947 us; the launch traced here: 938 us
  waiting for transfers between devices  571 us (60%)
  Pallas kernels  164 us (17%)
  matrix products  100 us (11%)
  blocking collectives  42 us (4%)
  other arithmetic  26.5 us (3%)
  local copies, waits for them, and re-layouts  15.6 us (2%)
  between operations  14.8 us (2%)
    reduce_scatter x4, waiting for transfers between devices, scatter(): lax.psum_scatter(grad.astype(bf16), both, scatter_dimension=0, tiled=True)  417 us
    pallas_call x1, Pallas kernels, local(): pl.pallas_call(functools.partial(local_kernel, chunk), grid=(heads,), in_...  86.5 us
    all_gather x1, waiting for transfers between devices, local(): lax.all_gather(jnp.concatenate([w_qkv, jnp.pad(w_beta, ((0, 0), (0, 128 -...  68.3 us
    all_gather x1, waiting for transfers between devices, local(): w_d = lax.all_gather(w_down, both, axis=0, tiled=True)  57 us
    psum x1, blocking collectives, local(): small = lax.psum((d_norm_gain, d_conv, d_head_gain[0], d_mlp_gain), both)  42 us
    dot_general x4, matrix products, nt(): lax.dot_general(a, b, (((1,), (1,)), ((), ())), precision=prec, preferred...  38.7 us
    dot_general x4, matrix products, nn(): lax.dot_general(a, b, (((1,), (0,)), ((), ())), precision=prec, preferred...  31.6 us
    pallas_call x1, Pallas kernels, local(): pl.pallas_call(functools.partial(back_kernel, chunk), grid=(heads,), in_s...  31.5 us
  transfers between devices with their start and end apart: 10, of which 7 were waited for; matrix products, arithmetic and copies ran while one was open for 11% of the time, Pallas kernels for 17%

profile of v1, /device:TPU:0, one launch (start us, length us, event | category | flops | bytes accessed | tf_op | source)
XLA Modules:
  0.0 938.5 jit_solution(6855434553099995083)
XLA Ops:
  7.2 0.8 copy.73
  8.0 1.6 fusion.27
  12.4 0.8 reduce-window.8
  13.6 1.5 fusion.13
  15.2 1.4 pad_convert_fusion.tq.tk.tv
  16.6 68.3 %all-gather.5.cloned.1.call-done = bf16[1024,3200]{1,0:T(8,128)(2,1)} async-done(((bf16[32,3200]{1,0:T(8,128)(2,1)}), bf16[1024,3200]{1,0:T(8,128)(2,1)}) %all-gather.5.cloned.1.call-update) | async-done | bytes 6553616 | tf_op jit(solution)/shard_map/all_gather | solution.py:323
  84.9 6.7 fusion.25.pq.pk.pv
  91.6 2.7 copy-done
  94.3 2.2 collective-permute-start
  98.1 0.9 copy.65.docs_c
  98.9 1.7 slice.72.logits
  101.3 86.5 %delta_local.1 = (f32[512,1024]{1,0:T(8,128)}, f32[512,1024]{1,0:T(8,128)}, f32[512,1024]{1,0:T(8,128)}, f32[512,1024]{1,0:T(8,128)}, f32[512,1024]{1,0:T(8,128)...) custom-call(f32[512,3200]{1,0:T(8,128)} %copy-done, ...), custom_call_target="tpu_custom_call" | custom-call | tf_op jit(solution)/shard_map/delta_local/pallas_call | solution.py:372
  187.8 1.6 copy.66
  189.4 1.0 copy.72
  190.4 1.0 copy.71
  191.4 5.8 relay.1.zin
  197.2 10.8 %delta_out.1 = (f32[512,1024]{1,0:T(8,128)}, f32[512,1024]{1,0:T(8,128)}, bf16[512,1024]{1,0:T(8,128)(2,1)}) custom-call(bf16[8,128,128]{2,1,0:T(8,128)(2,1)} %relay.1.zin, f32[512,1024]{1,0:T(8,128)} %get-tuple-element.42.dt.dt_r, f32[512,1024]{1,0:T(8,128)} %get-tuple-element.43.ft, f32[512,1024]{1,0:T(8,128)} %get-tuple-element.44.qt, ...), custom_call_target="tpu_custom_call" | custom-call | tf_op jit(solution)/shard_map/delta_out/pallas_call | solution.py:404
  208.0 3.3 multiply_reduce_fusion.2
  211.3 25.7 %all-gather.9.cloned.1.call-done = bf16[1024,5632]{1,0:T(8,128)(2,1)} async-done(((bf16[32,5632]{1,0:T(8,128)(2,1)}), bf16[1024,5632]{1,0:T(8,128)(2,1)}) %all-gather.9.cloned.1.call-update) | async-done | bytes 11534352 | tf_op jit(solution)/shard_map/all_gather | solution.py:327
  237.0 13.3 %fusion.38 = f32[512,5632]{1,0:T(8,128)} fusion(bf16[1024,5632]{1,0:T(8,128)(2,1)} %all-gather.9.cloned.1.call-done, f32[512,1024]{1,0:T(8,128)S(1)} %get-tuple-element.149, f32[1024]{0:T(1024)S(1)} %convert_element_type.90, f32[512]{0:T(512)S(1)} %fusion.29), kind=kOutput, calls=%fused_computation.83 | convolution fusion | flops 5907152896 | bytes 25171968 | tf_op jit(solution)/shard_map/dot_general | solution.py:19
  250.2 57.0 %all-gather.11.cloned.1.call-done = bf16[2816,1024]{1,0:T(8,128)(2,1)} async-done(((bf16[88,1024]{1,0:T(8,128)(2,1)}), bf16[2816,1024]{1,0:T(8,128)(2,1)}) %all-gather.11.cloned.1.call-update) | async-done | bytes 5767184 | tf_op jit(solution)/shard_map/all_gather | solution.py:328
  307.3 13.0 %fusion.19 = (f32[512,2816]{1,0:T(8,128)}, f32[512,2816]{1,0:T(8,128)}, bf16[512,2816]{1,0:T(8,128)(2,1)}) fusion(f32[512,5632]{1,0:T(8,128)} %fusion.38, bf16[512,1024]{1,0:T(8,128)(2,1)} %param.23, bf16[2816,1024]{1,0:T(8,128)(2,1)} %all-gather.11.cloned.1.call-done), kind=kOutput, calls=%fused_computation.39 | convolution fusion | flops 2972975104 | bytes 32768000 | tf_op jit(solution)/shard_map/dot_general | solution.py:23
  320.3 13.5 %multiply_reduce_fusion = (f32[1024]{0:T(1024)S(1)}, f32[512]{0:T(512)S(1)}, f32[512,1024]{1,0:T(8,128)}) fusion(f32[512,1024]{1,0:T(8,128)S(1)} %get-tuple-element.149, f32[512]{0:T(512)S(1)} %fusion.29, f32[1024]{0:T(1024)S(1)} %convert_element_type.90, bf16[1024,5632]{1,0:T(8,128)(2,1)} %all-gather.9.cloned.1.call-done, ...), kind=kOutput, calls=%fused_computation.31 | convolution fusion | flops 5914491392 | bytes 27275264 | tf_op jit(solution)/shard_map/dot_general | solution.py:23
  333.8 3.2 fusion.10
  337.0 2.6 convolution_convert_fusion.3
  339.9 7.8 convolution_convert_fusion.2
  347.8 4.2 fusion.21.dh
  352.0 10.7 %delta_seed.1 = (f32[512,1024]{1,0:T(8,128)}, f32[512,1024]{1,0:T(8,128)}, f32[8,128,128]{2,1,0:T(8,128)}, f32[8,128]{1,0:T(8,128)}) custom-call(f32[512,1024]{1,0:T(8,128)} %fusion.21.dh, f32[512,1024]{1,0:T(8,128)} %get-tuple-element.56.o, f32[1,128]{1,0:T(1,128)} %bitcast_convert_fusion.gain, f32[512,1024]{1,0:T(8,128)} %get-tuple-element.44.qt, ...), custom_call_target="tpu_custom_call" | custom-call | tf_op jit(solution)/shard_map/delta_seed/pallas_call | solution.py:430
  362.7 18.7 %relay_back.1.g_r = bf16[8,128,128]{2,1,0:T(8,128)(2,1)} custom-call(f32[8,128,128]{2,1,0:T(8,128)} %bitcast.39, f32[8,128,128]{2,1,0:T(8,128)} %get-tuple-element.59.add_ref), custom_call_target="tpu_custom_call" | custom-call | tf_op jit(solution)/shard_map/relay_back/pallas_call | solution.py:388
  381.4 31.5 %delta_back.1 = (f32[512,1024]{1,0:T(8,128)}, f32[512,1024]{1,0:T(8,128)}, f32[512,1024]{1,0:T(8,128)}, f32[8,1024]{1,0:T(8,128)}, f32[8,1024]{1,0:T(8,128)}, /*...) custom-call(f32[512,3200]{1,0:T(8,128)} %copy-done, ...), custom_call_target="tpu_custom_call" | custom-call | tf_op jit(solution)/shard_map/delta_back/pallas_call | solution.py:440
  415.2 1.3 collective-permute-start.1
  416.5 1.0 convert_element_type.98
  417.5 0.8 collective-permute-done.1
  418.3 3.7 fusion.1
  422.0 1.6 copy-done.3
  423.6 5.8 convolution_convert_fusion.1
  429.8 13.8 %convolution_convert_fusion = bf16[1024,5632]{1,0:T(8,128)(2,1)} fusion(f32[512,2816]{1,0:T(8,128)} %get-tuple-element.135, f32[512,2816]{1,0:T(8,128)} %get-tuple-element.134, f32[512,1024]{1,0:T(8,128)} %copy-done.1, f32[1024]{0:T(1024)S(1)} %convert_element_type.90, f32[512]{0:T(512)S(1)} %fusion.29), kind=kOutput, calls=%fused_computation.1 | convolution fusion | flops 5918687232 | bytes 25171968 | tf_op jit(solution)/shard_map/dot_general | solution.py:27
  444.4 8.4 add_convert_fusion.1
  452.8 8.0 fusion.9
  460.8 42.0 %all-reduce.7 = (f32[1024]{0:T(1024)}, f32[4,3072]{1,0:T(4,128)}, f32[128]{0:T(128)}, f32[1024]{0:T(1024)}) all-reduce(f32[1024]{0:T(1024)S(1)} %get-tuple-element.128, f32[4,3072]{1,0:T(4,128)S(1)} %pad_maximum_fusion, f32[128]{0:T(128)S(1)} %slice_bitcast_fusion.1, ...), channel_id=1, replica_groups=mesh['dp'=4,'seq'=8] {'dp','seq'}, use_global_device_ids=true, to_apply=%region_7.8 | all-reduce | flops 14464 | bytes 115712 | tf_op jit(solution)/shard_map/psum | solution.py:470
  502.8 3.1 fusion.12
  506.0 1.5 convert_element_type.103
  507.5 113.8 %reduce-scatter.11.cloned.1.call-done = bf16[88,1024]{1,0:T(8,128)(2,1)} async-done(((bf16[2816,1024]{1,0:T(8,128)(2,1)}), bf16[88,1024]{1,0:T(8,128)(2,1)}) %reduce-scatter.11.cloned.1.call-update) | async-done | bytes 180240 | tf_op jit(solution)/shard_map/reduce_scatter | solution.py:464
  621.2 1.7 convert_element_type.107
  622.9 145.9 %reduce-scatter.5.cloned.1.call-done = bf16[32,3200]{1,0:T(8,128)(2,1)} async-done(((bf16[1024,3200]{1,0:T(8,128)(2,1)}), bf16[32,3200]{1,0:T(8,128)(2,1)}) %reduce-scatter.5.cloned.1.call-update) | async-done | bytes 204816 | tf_op jit(solution)/shard_map/reduce_scatter | solution.py:464
  770.1 1.7 slice.77
  771.8 157.5 %reduce-scatter.9.cloned.1.call-done = bf16[32,5632]{1,0:T(8,128)(2,1)} async-done(((bf16[1024,5632]{1,0:T(8,128)(2,1)}), bf16[32,5632]{1,0:T(8,128)(2,1)}) %reduce-scatter.9.cloned.1.call-update) | async-done | bytes 360464 | tf_op jit(solution)/shard_map/reduce_scatter | solution.py:464
  929.3 1.9 convert_element_type.105
  (74 shorter events, 10.6 us)
Async XLA Ops:
  7.2 77.8 %all-gather.5.cloned.1.call-start = ((), (), s32[]{:S(2)}) async-start(), calls=%async_computation.4 | async-start | bytes 6758400 | tf_op jit(solution)/shard_map/all_gather | solution.py:323
  9.6 198.4 %all-gather.7.cloned.1.call-start = ((), (), s32[]{:S(2)}) async-start(), calls=%async_computation.5 | async-start | bytes 2162688 | tf_op jit(solution)/shard_map/all_gather | solution.py:326
  10.4 226.6 %all-gather.9.cloned.1.call-start = ((), (), s32[]{:S(2)}) async-start(), calls=%async_computation.6 | async-start | bytes 11894784 | tf_op jit(solution)/shard_map/all_gather | solution.py:327
  11.1 296.1 %all-gather.11.cloned.1.call-start = ((), (), s32[]{:S(2)}) async-start(), calls=%async_computation.7 | async-start | bytes 5947392 | tf_op jit(solution)/shard_map/all_gather | solution.py:328
  11.7 494.3 %reduce-scatter.7.cloned.1.call-start = ((), (), s32[]{:S(2)}) async-start(), calls=%async_computation.9 | async-start | bytes 2162688 | tf_op jit(solution)/shard_map/reduce_scatter | solution.py:464
  13.4 84.6 %copy-start.8 = (s32[512]{0:T(512)}, s32[512]{0:T(512)S(1)}, u32[]{:S(2)}) copy-start(s32[512]{0:T(512)S(1)} %get-tuple-element.139) | copy-start | bytes 6148
  16.6 79.9 %copy-start.11 = (bf16[128]{0:T(256)(128)(2,1)S(1)}, bf16[128]{0:T(256)(128)(2,1)}, u32[]{:S(2)}) copy-start(bf16[128]{0:T(256)(128)(2,1)} %param.18) | copy-start | bytes 772
  16.6 80.4 %copy-start.9 = (bf16[1024]{0:T(1024)(128)(2,1)S(1)}, bf16[1024]{0:T(1024)(128)(2,1)}, u32[]{:S(2)}) copy-start(bf16[1024]{0:T(1024)(128)(2,1)} %param.20) | copy-start | bytes 6148
  91.6 2.7 copy-start
  94.3 6.3 collective-permute-start
  197.2 10.8 %copy-start.2 = (bf16[512,1024]{1,0:T(8,128)(2,1)S(1)}, bf16[512,1024]{1,0:T(8,128)(2,1)}, u32[]{:S(2)}) copy-start(bf16[512,1024]{1,0:T(8,128)(2,1)} %param.12) | copy-start | bytes 3145732
  211.3 109.0 %copy-start.1 = (f32[512,1024]{1,0:T(8,128)}, f32[512,1024]{1,0:T(8,128)S(1)}, u32[]{:S(2)}) copy-start(f32[512,1024]{1,0:T(8,128)S(1)} %get-tuple-element.149) | copy-start | bytes 6291460
  333.8 3.2 copy-start.10
  339.6 281.6 %reduce-scatter.11.cloned.1.call-start = ((), (), s32[]{:S(2)}) async-start(), calls=%async_computation.11 | async-start | bytes 5947392 | tf_op jit(solution)/shard_map/reduce_scatter | solution.py:464
  347.7 421.1 %reduce-scatter.5.cloned.1.call-start = ((), (), s32[]{:S(2)}) async-start(), calls=%async_computation.8 | async-start | bytes 6758400 | tf_op jit(solution)/shard_map/reduce_scatter | solution.py:464
  415.2 3.1 collective-permute-start.1
  422.0 1.6 copy-start.3
  429.5 499.8 %reduce-scatter.9.cloned.1.call-start = ((), (), s32[]{:S(2)}) async-start(), calls=%async_computation.10 | async-start | bytes 11894784 | tf_op jit(solution)/shard_map/reduce_scatter | solution.py:464
  443.6 0.8 copy-start.5
  443.6 0.8 copy-start.6
  443.6 0.8 copy-start.7
  444.4 8.4 copy-start.4
Sparse Core Ops, SparseCore 0:
  11.4 73.4 all-gather.4
  87.9 55.3 all-gather.6
  146.2 90.7 all-gather.8
  239.7 67.5 all-gather.10
  339.7 136.0 reduce-scatter.6
  478.1 143.1 reduce-scatter.10
  623.6 145.0 reduce-scatter.4
  771.2 158.0 reduce-scatter.8
